TPU v7x, 512 devices: a whole 4x4x16 slice. The times are simulated.
512 devices in a mesh: gx: 32 (over z, core), gy: 16 (over y, x).
Axes of the slice: x: 4, y: 4, z: 16, core: 2. Of those that a mesh axis runs over, the one named last changes fastest.
Arguments:
- solution: float32 [512, 65536], P(None, ('gx', 'gy')), may hold values from -6 to 6
- residual: float32 [512, 65536], P(None, ('gx', 'gy')), may hold values from -60 to 60
- metric_diag: bfloat16 [3, 512, 65536], P(None, None, ('gx', 'gy')), may hold values from 0.039794922 to 0.3984375
- metric_cross: bfloat16 [3, 512, 65536], P(None, None, ('gx', 'gy')), may hold values from -0.017944336 to 0.017944336
- fdm_vectors: float32 [3, 8, 8, 65536], P(None, None, None, ('gx', 'gy')), may hold values from -5 to 5
- fdm_values: float32 [3, 8, 65536], P(None, None, ('gx', 'gy')), may hold values from 0.05 to 20
- vertex_ids: int32 [8, 65536], P(None, ('gx', 'gy')), may hold values from 0 to 8191
- coarse_inverse: float32 [8192, 8192], P(('gx', 'gy')), may hold values from -0.2 to 0.2, as said below
- elem_live: int32 [512], P(('gx', 'gy')), may hold values from 80 to 128, as said below
- section_face: int32 [512, 16, 20], P(('gx', 'gy')), may hold values from -1 to 767, as said below
- section_code: int32 [512, 16, 20], P(('gx', 'gy')), may hold values from 0 to 7, as said below
- pipe_face: int32 [512, 2, 64], P(('gx', 'gy')), may hold values from 0 to 767, as said below
- pipe_code: int32 [512, 2, 64], P(('gx', 'gy')), may hold values from 0 to 7, as said below
Outputs:
- solution_out: float32 [512, 65536], P(None, ('gx', 'gy'))
- residual_out: float32 [512, 65536], P(None, ('gx', 'gy'))
- norm_ratio: float32 [1], replicated
Inputs may be any that keep to these rules, and one draw needn't show every extreme that they name: `elem_live`: one device holds all 128 slots in every draw. A face id 6 e + f names face f of slot e of the device, with e below the device's elem_live; no id appears twice on a device over section_face and pipe_face; -1 marks an empty slot, and in each peer's row the slots holding faces come first. Slot (q, c) of device (x, y) holds a face exactly when slot (y, c) of device (x, q) does; in the row q = y they come in pairs (c, c xor 1). Each device's rows for peers y - 1, y + 1 and y + 16 / 2 (mod 16) are full; rows for other peers more than two places away (mod 16) are empty. `section_code`: with inv(o) = o for o < 4 and 4 + 2 (o mod 2) + floor((o mod 4) / 2) for o >= 4, the codes of two paired slots are inv of each other; empty slots hold 0. `pipe_face`: every slot holds a face, as for section_face. `pipe_code`: the codes of two paired slots are inv of each other, as for section_code. `coarse_inverse`: Symmetric.
All inputs are finite; a program needn't handle non-finite values.
Results may differ from a plain program's by a relative error of at most 0.0003.
Values sent between devices are 32-bit elements; how exact they have to be, the bound alone decides.
A program may use at most 64 MiB of HBM per device.

v0:
```python
import jax
import jax.numpy as jnp
from jax import lax
from jax.sharding import PartitionSpec as P

EDGE = 8
top_precision = lax.Precision.HIGHEST


def padded(block, sides, width):
    for axis, dim in sides:
        count = lax.axis_size(axis)
        forward = [(i, i + 1) for i in range(count - 1)]
        forward.append((count - 1, 0))
        backward = [(target, source) for source, target in forward]
        low = lax.ppermute(
            lax.slice_in_dim(block, block.shape[dim] - width, None, axis=dim), axis, forward
        )
        high = lax.ppermute(lax.slice_in_dim(block, 0, width, axis=dim), axis, backward)
        block = jnp.concatenate([low, block, high], axis=dim)
    return block


def node_points():
    node_index = jnp.arange(EDGE).astype(jnp.float32)
    return -jnp.cos(jnp.pi * node_index / (EDGE - 1))


def derivative_matrix():
    points = node_points()
    node_index = jnp.arange(EDGE)
    weights = jnp.where((node_index == 0) | (node_index == EDGE - 1), 2.0, 1.0).astype(jnp.float32)
    parity = jnp.where((node_index[:, None] + node_index[None, :]) % 2 == 0, 1.0, -1.0).astype(
        jnp.float32
    )
    identity = jnp.eye(EDGE, dtype=jnp.float32)
    spacing = points[:, None] - points[None, :] + identity
    offdiag = weights[:, None] / weights[None, :] * parity / spacing * (1.0 - identity)
    return offdiag - jnp.diag(jnp.sum(offdiag, axis=1))


def corner_table():
    points = node_points()
    hat_values = jnp.stack([(1.0 - points) * 0.5, (1.0 + points) * 0.5])
    corner_weights = (
        hat_values[:, None, None, :, None, None]
        * hat_values[None, :, None, None, :, None]
        * hat_values[None, None, :, None, None, :]
    )
    return corner_weights.reshape(8, EDGE**3)


def contract(matrices, element_cube, axis):
    moved = jnp.moveaxis(element_cube, axis, 0)
    total = matrices[0][:, None, None, :] * moved[0][None]
    for index in range(1, EDGE):
        total = total + matrices[index][:, None, None, :] * moved[index][None]
    return jnp.moveaxis(total, 0, axis)


def orient_columns(face_cols, orient_codes):
    face_grid = face_cols.reshape(EDGE, EDGE, -1)
    face_grid = jnp.where((orient_codes % 2 == 1)[None, None, :], face_grid[::-1, :, :], face_grid)
    face_grid = jnp.where(
        (orient_codes // 2 % 2 == 1)[None, None, :], face_grid[:, ::-1, :], face_grid
    )
    face_grid = jnp.where(
        (orient_codes >= 4)[None, None, :], jnp.swapaxes(face_grid, 0, 1), face_grid
    )
    return face_grid.reshape(EDGE * EDGE, -1)


def fdm_solve(element_cube, vectors, values):
    spectral = contract(vectors[0], element_cube, 0)
    spectral = contract(vectors[1], spectral, 1)
    spectral = contract(vectors[2], spectral, 2)
    eigen_sums = (
        values[0][:, None, None, :] + values[1][None, :, None, :] + values[2][None, None, :, :]
    )
    spectral = spectral / eigen_sums
    restored = contract(jnp.swapaxes(vectors[0], 0, 1), spectral, 0)
    restored = contract(jnp.swapaxes(vectors[1], 0, 1), restored, 1)
    return contract(jnp.swapaxes(vectors[2], 0, 1), restored, 2)


def local_operator(field, diag_part, cross_part, derivative):
    element_cube = field.reshape(EDGE, EDGE, EDGE, -1)
    diagonal = diag_part.astype(jnp.float32).reshape(3, EDGE, EDGE, EDGE, -1)
    cross_terms = cross_part.astype(jnp.float32).reshape(3, EDGE, EDGE, EDGE, -1)
    forward = jnp.transpose(derivative)[:, :, None]
    backward = derivative[:, :, None]
    grad_first = contract(forward, element_cube, 0)
    grad_second = contract(forward, element_cube, 1)
    grad_third = contract(forward, element_cube, 2)
    flux_first = (
        diagonal[0] * grad_first + cross_terms[0] * grad_second + cross_terms[1] * grad_third
    )
    flux_second = (
        cross_terms[0] * grad_first + diagonal[1] * grad_second + cross_terms[2] * grad_third
    )
    flux_third = (
        cross_terms[1] * grad_first + cross_terms[2] * grad_second + diagonal[2] * grad_third
    )
    curvature = jnp.sum(
        grad_first * flux_first + grad_second * flux_second + grad_third * flux_third
    ) + jnp.sum(element_cube * element_cube)
    applied = contract(backward, flux_first, 0)
    applied = applied + contract(backward, flux_second, 1)
    applied = applied + contract(backward, flux_third, 2)
    return ((applied + element_cube).reshape(EDGE**3, -1), curvature)


def face_sum(field, section_face, section_code, pipe_face, pipe_code):
    element_cube = field.reshape(EDGE, EDGE, EDGE, -1)
    slot_count = element_cube.shape[3]
    stacked = jnp.stack(
        [
            element_cube[0],
            element_cube[EDGE - 1],
            element_cube[:, 0],
            element_cube[:, EDGE - 1],
            element_cube[:, :, 0],
            element_cube[:, :, EDGE - 1],
        ],
        axis=-1,
    )
    face_values = stacked.reshape(EDGE * EDGE, slot_count * 6)
    face_count = face_values.shape[1]
    peer_count = section_face.shape[1]
    capacity = section_face.shape[2]
    wanted = section_face[0].reshape(-1)
    picked = jnp.take(face_values, jnp.maximum(wanted, 0), axis=1)
    outgoing = jnp.where((wanted >= 0)[None, :], picked, 0.0).reshape(
        EDGE * EDGE, peer_count, capacity
    )
    own_index = lax.axis_index("gy")
    arrived = lax.all_to_all(outgoing, "gy", split_axis=1, concat_axis=1, tiled=True)
    swapped = arrived.reshape(EDGE * EDGE, peer_count, capacity // 2, 2)[..., ::-1].reshape(
        EDGE * EDGE, peer_count, capacity
    )
    arrived = jnp.where((jnp.arange(peer_count) == own_index)[None, :, None], swapped, arrived)
    incoming = orient_columns(
        arrived.reshape(EDGE * EDGE, peer_count * capacity), section_code[0].reshape(-1)
    )
    pipe_ids = pipe_face[0]
    pipe_width = pipe_ids.shape[1]
    boundary = jnp.take(face_values, pipe_ids.reshape(-1), axis=1).reshape(
        EDGE * EDGE, 2, pipe_width
    )
    extended = padded(boundary, (("gx", 1),), 1)
    beside = jnp.concatenate([extended[:, 0], extended[:, 3]], axis=1)
    beside = orient_columns(beside, pipe_code[0].reshape(-1))
    targets = jnp.concatenate([wanted, pipe_ids.reshape(-1)])
    placed = jnp.where(targets < 0, face_count, targets)
    face_extra = (
        jnp.zeros((EDGE * EDGE, face_count), jnp.float32)
        .at[:, placed]
        .add(jnp.concatenate([incoming, beside], axis=1), mode="drop")
    )
    face_parts = face_extra.reshape(EDGE, EDGE, slot_count, 6)
    element_cube = element_cube.at[0].add(face_parts[..., 0])
    element_cube = element_cube.at[EDGE - 1].add(face_parts[..., 1])
    element_cube = element_cube.at[:, 0].add(face_parts[..., 2])
    element_cube = element_cube.at[:, EDGE - 1].add(face_parts[..., 3])
    element_cube = element_cube.at[:, :, 0].add(face_parts[..., 4])
    element_cube = element_cube.at[:, :, EDGE - 1].add(face_parts[..., 5])
    return element_cube.reshape(EDGE**3, -1)


def on_device(
    solution,
    residual,
    metric_diag,
    metric_cross,
    fdm_vectors,
    fdm_values,
    vertex_ids,
    coarse_inverse,
    elem_live,
    section_face,
    section_code,
    pipe_face,
    pipe_code,
):
    slot_count = residual.shape[1]
    alive_mask = (jnp.arange(slot_count) < elem_live[0]).astype(jnp.float32)
    rmask = residual * alive_mask[None, :]
    corner_weights = corner_table()
    derivative = derivative_matrix()
    corners = jnp.dot(corner_weights, rmask, precision=top_precision)
    coarse_partial = jax.ops.segment_sum(
        corners.reshape(-1), vertex_ids.reshape(-1), num_segments=coarse_inverse.shape[1]
    )
    coarse_rhs = lax.psum(coarse_partial, ("gx", "gy"))
    own_values = jnp.dot(coarse_inverse, coarse_rhs, precision=top_precision)
    coarse_sol = lax.all_gather(own_values, ("gx", "gy"), axis=0, tiled=True)
    smooth = fdm_solve(rmask.reshape(EDGE, EDGE, EDGE, -1), fdm_vectors, fdm_values).reshape(
        EDGE**3, -1
    )
    summed = face_sum(smooth, section_face, section_code, pipe_face, pipe_code)
    lifted = jnp.dot(corner_weights.T, coarse_sol[vertex_ids], precision=top_precision)
    direction = alive_mask[None, :] * (summed + lifted)
    applied, curvature_local = local_operator(direction, metric_diag, metric_cross, derivative)
    image = face_sum(applied, section_face, section_code, pipe_face, pipe_code)
    precond_local = jnp.sum(rmask * direction)
    norm_local = jnp.sum(rmask * rmask)
    precond_dot, curvature, old_norm = lax.psum(
        (precond_local, curvature_local, norm_local), ("gx", "gy")
    )
    step_length = precond_dot / curvature
    residual_out = rmask - step_length * image
    fresh_norm = lax.psum(jnp.sum(residual_out * residual_out), ("gx", "gy"))
    solution_out = alive_mask[None, :] * (solution + step_length * direction)
    norm_ratio = (fresh_norm / old_norm).reshape(1)
    return (solution_out, residual_out, norm_ratio)


def solution(mesh):
    placed = (
        P(None, ("gx", "gy")),
        P(None, ("gx", "gy")),
        P(None, None, ("gx", "gy")),
        P(None, None, ("gx", "gy")),
        P(None, None, None, ("gx", "gy")),
        P(None, None, ("gx", "gy")),
        P(None, ("gx", "gy")),
        P(("gx", "gy"), None),
        P(("gx", "gy")),
        P(("gx", "gy"), None, None),
        P(("gx", "gy"), None, None),
        P(("gx", "gy"), None, None),
        P(("gx", "gy"), None, None),
    )
    return jax.shard_map(
        on_device,
        mesh=mesh,
        in_specs=placed,
        out_specs=(P(None, ("gx", "gy")), P(None, ("gx", "gy")), P()),
        check_vma=False,
    )
```

profile of v0, /device:TPU:1, one launch (start us, length us, event | category | flops | bytes accessed | tf_op | source)
XLA Modules:
  0.0 567.3 jit_solution(12377010773833954774)
XLA Ops:
  0.7 0.9 slice_bitcast_fusion.120
  2.3 0.8 slice_bitcast_fusion.92
  3.8 1.0 broadcast_multiply_fusion.3
  6.8 2.3 copy.389
  9.0 2.5 reshape.1869
  12.5 1.1 gather_fusion.1
  14.6 7.6 %all-to-all-start = ((f32[16,1,1280]{2,1,0:T(1,128)}), f32[16,1,1280]{2,1,0:T(1,128)}, u32[]{:S(2)}, u32[]{:S(2)}) async-start(f32[16,1,1280]{2,1,0:T(1,128)} %reshape.1990), calls=%async_computation | async-start | bytes 163840 | tf_op jit(solution)/shard_map/all_to_all | solution.py:137
  23.7 2.5 collective-permute-start
  26.8 0.9 collective-permute-start.1
  30.1 5.9 %scatter_custom_fusion.1 = f32[8192]{0:T(1024)S(1)} fusion(s32[1024]{0:T(1024)S(1)} %bitcast.649, f32[1024]{0:T(1024)S(1)} %convolution_bitcast_fusion, f32[]{:T(128)} %constant.402.clone.1), kind=kCustom, calls=%fused_computation.199 | custom fusion | flops 1024 | bytes 32772 | tf_op jit(solution)/shard_map/scatter-add | solution.py:191
  36.1 108.5 %psum.35 = f32[8192]{0:T(1024)S(1)} all-reduce(f32[8192]{0:T(1024)S(1)} %scatter_custom_fusion.1), channel_id=1, replica_groups=mesh['gx'=32,'gy'=16] {'gx','gy'}, use_global_device_ids=true, to_apply=%region_2.5 | all-reduce | flops 8192 | bytes 65536 | tf_op jit(solution)/shard_map/psum | solution.py:194
  145.0 1.0 fusion.56
  145.9 1.0 fusion.55
  169.9 99.5 %all-reduce = f32[8192]{0:T(1024)S(1)} all-reduce(f32[8192]{0:T(1024)S(1)} %dynamic-update-slice.36), channel_id=1, replica_groups=mesh['gx'=32,'gy'=16] {'gx','gy'}, use_global_device_ids=true, to_apply=%add | all-reduce | flops 8192 | bytes 65536
  269.4 10.5 %gather_fusion = f32[1024]{0:T(1024)} fusion(f32[8192]{0:T(1024)S(1)} %all-reduce, s32[1024]{0:T(1024)S(1)} %fusion.40), kind=kCustom, calls=%fused_computation.4 | custom fusion | bytes 12288 | tf_op jit(solution)/shard_map/gather | solution.py:201
  280.6 1.6 reduce.26
  283.5 2.3 scatter_custom_fusion
  285.7 2.6 reshape.1876
  288.4 3.4 fusion.54
  291.8 1.9 copy.456
  293.6 0.8 copy.457
  294.4 1.3 copy.401
  295.7 1.2 copy.403
  296.9 1.2 copy.458
  298.1 1.2 copy.459
  299.4 0.9 fusion.25
  301.8 2.0 multiply_reduce_fusion
  304.4 1.5 multiply_add_fusion
  306.1 1.5 add_bitcast_fusion.1
  309.7 2.3 copy.428
  312.0 2.4 reshape.1886
  314.4 1.1 gather_fusion.3
  317.3 4.2 all-to-all-start.1
  322.3 1.8 collective-permute-start.2
  324.9 0.8 mul.2645
  325.9 0.8 mul.2653
  326.7 0.8 mul.2661
  339.6 2.9 add_reduce_fusion
  343.7 102.5 %all-reduce.2 = (f32[]{:T(128)}, f32[]{:T(128)}) all-reduce(f32[]{:T(128)} %get-tuple-element.150, f32[]{:T(128)S(6)} %add.970), channel_id=1, replica_groups=mesh['gx'=32,'gy'=16] {'gx','gy'}, use_global_device_ids=true, to_apply=%region_4.7 | all-reduce | flops 2 | bytes 16 | tf_op jit(solution)/shard_map/psum | solution.py:207
  447.6 1.7 add_multiply_fusion
  449.3 0.9 pad_maximum_fusion.1
  450.2 1.6 reduce.27
  453.1 2.5 scatter_custom_fusion.2
  455.7 2.6 reshape.1893
  458.3 2.9 fusion.53
  461.2 1.2 copy.462
  464.1 1.3 multiply_reduce_fusion.1
  465.4 99.4 %all-reduce.1 = (f32[]{:T(128)}, f32[]{:T(128)}) all-reduce(f32[]{:T(128)} %get-tuple-element.156, f32[]{:T(128)} %get-tuple-element.149), channel_id=1, replica_groups=mesh['gx'=32,'gy'=16] {'gx','gy'}, use_global_device_ids=true, to_apply=%region_11.14 | all-reduce | flops 2 | bytes 16 | tf_op jit(solution)/shard_map/psum | solution.py:212
  (499 shorter events, 55.4 us)
Async XLA Ops:
  0.6 147.6 %copy-start = (f32[16,8192]{1,0:T(8,128)S(1)}, f32[16,8192]{1,0:T(8,128)}, u32[]{:S(2)}) copy-start(f32[16,8192]{1,0:T(8,128)} %param.48) | copy-start | bytes 1572868
  9.0 13.9 %copy-start.124 = (s32[1,2,64]{2,1,0:T(2,128)S(1)}, s32[1,2,64]{2,1,0:T(2,128)}, u32[]{:S(2)}) copy-start(s32[1,2,64]{2,1,0:T(2,128)} %param.53) | copy-start | bytes 1540
  9.0 21.1 %copy-start.121 = (s32[8,128]{1,0:T(8,128)S(1)}, s32[8,128]{1,0:T(8,128)}, u32[]{:S(2)}) copy-start(s32[8,128]{1,0:T(8,128)} %param.47) | copy-start | bytes 12292
  9.0 135.9 %copy-start.2 = (bf16[3,512,128]{2,1,0:T(8,128)(2,1)S(1)}, bf16[3,512,128]{2,1,0:T(8,128)(2,1)}, u32[]{:S(2)}) copy-start(bf16[3,512,128]{2,1,0:T(8,128)(2,1)} %param.44) | copy-start | bytes 1179652
  11.5 134.5 %copy-start.1 = (bf16[3,512,128]{2,1,0:T(8,128)(2,1)S(1)}, bf16[3,512,128]{2,1,0:T(8,128)(2,1)}, u32[]{:S(2)}) copy-start(bf16[3,512,128]{2,1,0:T(8,128)(2,1)} %param.43) | copy-start | bytes 1179652
  12.5 134.4 %copy-start.110 = (s32[1024]{0:T(1024)}, s32[1024]{0:T(1024)S(1)}, u32[]{:S(2)}) copy-start(s32[1024]{0:T(1024)S(1)} %get-tuple-element.373) | copy-start | bytes 12292
  14.6 265.5 %all-to-all-start = ((f32[16,1,1280]{2,1,0:T(1,128)}), f32[16,1,1280]{2,1,0:T(1,128)}, u32[]{:S(2)}, u32[]{:S(2)}) async-start(f32[16,1,1280]{2,1,0:T(1,128)} %reshape.1990), calls=%async_computation | async-start | bytes 163840 | tf_op jit(solution)/shard_map/all_to_all | solution.py:137
  23.5 256.5 %copy-start.66 = (pred[128]{0:T(512)(128)(4,1)}, pred[128]{0:T(512)(128)(4,1)S(1)}, u32[]{:S(2)}) copy-start(pred[128]{0:T(512)(128)(4,1)S(1)} %get-tuple-element.360) | copy-start | bytes 388
  23.7 256.2 %collective-permute-start = (f32[64,1,64]{2,0,1:T(8,128)S(1)}, f32[64,1,64]{2,0,1:T(8,128)S(1)}, u32[]{:S(2)}, u32[]{:S(2)}) collective-permute-start(f32[64,1,64]{2,0,1:T(8,128)S(1)} %copy.454), channel_id=1, source_target_pairs={{0,16},{16,32},{32,48},{48,64},{64,80},{80,96},{96,112},{112,128},... | collective-permute-start | bytes 49160 | tf_op jit(solution)/shard_map/ppermute | solution.py:16
  26.8 253.1 %collective-permute-start.1 = (f32[64,1,64]{2,0,1:T(8,128)}, f32[64,1,64]{2,0,1:T(8,128)S(1)}, u32[]{:S(2)}, u32[]{:S(2)}) collective-permute-start(f32[64,1,64]{2,0,1:T(8,128)} %copy.455), channel_id=1, source_target_pairs={{16,0},{32,16},{48,32},{64,48},{80,64},{96,80},{112,96},{128,112},... | collective-permute-start | bytes 49160 | tf_op jit(solution)/shard_map/ppermute | solution.py:19
  144.9 19.5 %copy-start.42 = (f32[8]{0:T(128)}, f32[8]{0:T(128)S(1)}, u32[]{:S(2)}) copy-start(f32[8]{0:T(128)S(1)} %get-tuple-element.346) | copy-start | bytes 100
  144.9 20.1 %copy-start.56 = (f32[8]{0:T(128)}, f32[8]{0:T(128)S(1)}, u32[]{:S(2)}) copy-start(f32[8]{0:T(128)S(1)} %get-tuple-element.353) | copy-start | bytes 100
  144.9 20.8 %copy-start.54 = (f32[8]{0:T(128)}, f32[8]{0:T(128)S(1)}, u32[]{:S(2)}) copy-start(f32[8]{0:T(128)S(1)} %get-tuple-element.352) | copy-start | bytes 100
  144.9 21.4 %copy-start.52 = (f32[8]{0:T(128)}, f32[8]{0:T(128)S(1)}, u32[]{:S(2)}) copy-start(f32[8]{0:T(128)S(1)} %get-tuple-element.351) | copy-start | bytes 100
  144.9 22.1 %copy-start.50 = (f32[8]{0:T(128)}, f32[8]{0:T(128)S(1)}, u32[]{:S(2)}) copy-start(f32[8]{0:T(128)S(1)} %get-tuple-element.350) | copy-start | bytes 100
  144.9 22.8 %copy-start.48 = (f32[8]{0:T(128)}, f32[8]{0:T(128)S(1)}, u32[]{:S(2)}) copy-start(f32[8]{0:T(128)S(1)} %get-tuple-element.349) | copy-start | bytes 100
  144.9 23.5 %copy-start.46 = (f32[8]{0:T(128)}, f32[8]{0:T(128)S(1)}, u32[]{:S(2)}) copy-start(f32[8]{0:T(128)S(1)} %get-tuple-element.348) | copy-start | bytes 100
  145.0 24.1 %copy-start.44 = (f32[8]{0:T(128)}, f32[8]{0:T(128)S(1)}, u32[]{:S(2)}) copy-start(f32[8]{0:T(128)S(1)} %get-tuple-element.347) | copy-start | bytes 100
  152.5 127.5 %copy-start.83 = (pred[128]{0:T(512)(128)(4,1)S(1)}, pred[128]{0:T(512)(128)(4,1)}, u32[]{:S(2)}) copy-start(pred[128]{0:T(512)(128)(4,1)} %get-tuple-element.361) | copy-start | bytes 388
  152.6 127.5 %copy-start.117 = (pred[128]{0:T(512)(128)(4,1)S(1)}, pred[128]{0:T(512)(128)(4,1)}, u32[]{:S(2)}) copy-start(pred[128]{0:T(512)(128)(4,1)} %get-tuple-element.359) | copy-start | bytes 388
  165.0 117.4 %copy-start.122 = (pred[16]{0:T(512)(128)(4,1)S(1)}, pred[16]{0:T(512)(128)(4,1)}, u32[]{:S(2)}) copy-start(pred[16]{0:T(512)(128)(4,1)} %iota_compare_fusion.2) | copy-start | bytes 52
  269.4 13.6 %copy-start.64 = (pred[320]{0:T(512)(128)(4,1)S(1)}, pred[320]{0:T(512)(128)(4,1)}, u32[]{:S(2)}) copy-start(pred[320]{0:T(512)(128)(4,1)} %get-tuple-element.355) | copy-start | bytes 964
  269.4 13.8 %copy-start.73 = (pred[320]{0:T(512)(128)(4,1)S(1)}, pred[320]{0:T(512)(128)(4,1)}, u32[]{:S(2)}) copy-start(pred[320]{0:T(512)(128)(4,1)} %get-tuple-element.356) | copy-start | bytes 964
  269.4 13.8 %copy-start.111 = (pred[320]{0:T(512)(128)(4,1)S(1)}, pred[320]{0:T(512)(128)(4,1)}, u32[]{:S(2)}) copy-start(pred[320]{0:T(512)(128)(4,1)} %get-tuple-element.354) | copy-start | bytes 964
  317.3 132.9 %all-to-all-start.1 = ((f32[16,1,1280]{2,1,0:T(1,128)}), f32[16,1,1280]{2,1,0:T(1,128)}, u32[]{:S(2)}, u32[]{:S(2)}) async-start(f32[16,1,1280]{2,1,0:T(1,128)} %reshape.1992), calls=%async_computation.1 | async-start | bytes 163840 | tf_op jit(solution)/shard_map/all_to_all | solution.py:137
  321.4 17.7 %copy-start.19 = (f32[1,8,8,128]{3,0,2,1:T(1,128)S(1)}, f32[1,8,8,128]{3,0,2,1:T(1,128)}, u32[]{:S(2)}) copy-start(f32[1,8,8,128]{3,0,2,1:T(1,128)} %copy-done.18) | copy-start | bytes 98308
  322.3 127.0 %collective-permute-start.2 = (f32[64,1,64]{2,0,1:T(8,128)}, f32[64,1,64]{2,0,1:T(8,128)}, u32[]{:S(2)}, u32[]{:S(2)}) collective-permute-start(f32[64,1,64]{2,0,1:T(8,128)} %copy.460), channel_id=1, source_target_pairs={{0,16},{16,32},{32,48},{48,64},{64,80},{80,96},{96,112},{112,128},... | collective-permute-start | bytes 49160 | tf_op jit(solution)/shard_map/ppermute | solution.py:16
  324.1 15.1 %copy-start.17 = (f32[1,8,8,128]{3,0,2,1:T(1,128)S(1)}, f32[1,8,8,128]{3,0,2,1:T(1,128)}, u32[]{:S(2)}) copy-start(f32[1,8,8,128]{3,0,2,1:T(1,128)} %copy-done.16) | copy-start | bytes 98308
  324.8 124.5 %collective-permute-start.3 = (f32[64,1,64]{2,0,1:T(8,128)}, f32[64,1,64]{2,0,1:T(8,128)}, u32[]{:S(2)}, u32[]{:S(2)}) collective-permute-start(f32[64,1,64]{2,0,1:T(8,128)} %copy.461), channel_id=1, source_target_pairs={{16,0},{32,16},{48,32},{64,48},{80,64},{96,80},{112,96},{128,112},... | collective-permute-start | bytes 49160 | tf_op jit(solution)/shard_map/ppermute | solution.py:19
  324.8 14.4 %copy-start.15 = (f32[1,8,8,128]{3,0,2,1:T(1,128)S(1)}, f32[1,8,8,128]{3,0,2,1:T(1,128)}, u32[]{:S(2)}) copy-start(f32[1,8,8,128]{3,0,2,1:T(1,128)} %copy-done.14) | copy-start | bytes 98308
  324.9 14.4 %copy-start.13 = (f32[1,8,8,128]{3,0,2,1:T(1,128)S(1)}, f32[1,8,8,128]{3,0,2,1:T(1,128)}, u32[]{:S(2)}) copy-start(f32[1,8,8,128]{3,0,2,1:T(1,128)} %copy-done.12) | copy-start | bytes 98308
  325.7 13.6 %copy-start.86 = (f32[512]{0:T(512)S(1)}, f32[512]{0:T(512)}, u32[]{:S(2)}) copy-start(f32[512]{0:T(512)} %mul.2626) | copy-start | bytes 6148
  325.7 13.6 %copy-start.87 = (f32[512]{0:T(512)S(1)}, f32[512]{0:T(512)}, u32[]{:S(2)}) copy-start(f32[512]{0:T(512)} %mul.2634) | copy-start | bytes 6148
  325.7 13.6 %copy-start.88 = (f32[512]{0:T(512)S(1)}, f32[512]{0:T(512)}, u32[]{:S(2)}) copy-start(f32[512]{0:T(512)} %mul.2642) | copy-start | bytes 6148
  325.7 13.6 %copy-start.89 = (f32[512]{0:T(512)S(1)}, f32[512]{0:T(512)}, u32[]{:S(2)}) copy-start(f32[512]{0:T(512)} %mul.2650) | copy-start | bytes 6148
  325.7 13.6 %copy-start.90 = (f32[512]{0:T(512)S(1)}, f32[512]{0:T(512)}, u32[]{:S(2)}) copy-start(f32[512]{0:T(512)} %mul.2658) | copy-start | bytes 6148
  325.7 13.6 %copy-start.91 = (f32[512]{0:T(512)S(1)}, f32[512]{0:T(512)}, u32[]{:S(2)}) copy-start(f32[512]{0:T(512)} %mul.2666) | copy-start | bytes 6148
  325.7 13.6 %copy-start.92 = (f32[512]{0:T(512)S(1)}, f32[512]{0:T(512)}, u32[]{:S(2)}) copy-start(f32[512]{0:T(512)} %mul.2674) | copy-start | bytes 6148
  325.7 13.6 %copy-start.93 = (f32[512]{0:T(512)S(1)}, f32[512]{0:T(512)}, u32[]{:S(2)}) copy-start(f32[512]{0:T(512)} %mul.2682) | copy-start | bytes 6148
  325.7 13.6 %copy-start.94 = (f32[512]{0:T(512)S(1)}, f32[512]{0:T(512)}, u32[]{:S(2)}) copy-start(f32[512]{0:T(512)} %mul.2690) | copy-start | bytes 6148
  339.5 108.0 %copy-start.72 = (f32[128]{0:T(128)S(1)}, f32[128]{0:T(128)}, u32[]{:S(2)}) copy-start(f32[128]{0:T(128)} %copy-done.71) | copy-start | bytes 1540
  339.5 110.6 %copy-start.67 = (pred[128]{0:T(512)(128)(4,1)S(1)}, pred[128]{0:T(512)(128)(4,1)}, u32[]{:S(2)}) copy-start(pred[128]{0:T(512)(128)(4,1)} %copy-done.66) | copy-start | bytes 388
  339.6 110.6 %copy-start.84 = (pred[128]{0:T(512)(128)(4,1)S(1)}, pred[128]{0:T(512)(128)(4,1)}, u32[]{:S(2)}) copy-start(pred[128]{0:T(512)(128)(4,1)} %get-tuple-element.361) | copy-start | bytes 388
  339.6 110.6 %copy-start.118 = (pred[128]{0:T(512)(128)(4,1)S(1)}, pred[128]{0:T(512)(128)(4,1)}, u32[]{:S(2)}) copy-start(pred[128]{0:T(512)(128)(4,1)} %get-tuple-element.359) | copy-start | bytes 388
  339.6 112.4 %copy-start.123 = (pred[16]{0:T(512)(128)(4,1)S(1)}, pred[16]{0:T(512)(128)(4,1)}, u32[]{:S(2)}) copy-start(pred[16]{0:T(512)(128)(4,1)} %iota_compare_fusion.2) | copy-start | bytes 52
  342.5 110.2 %copy-start.65 = (pred[320]{0:T(512)(128)(4,1)S(1)}, pred[320]{0:T(512)(128)(4,1)}, u32[]{:S(2)}) copy-start(pred[320]{0:T(512)(128)(4,1)} %get-tuple-element.355) | copy-start | bytes 964
  342.5 110.4 %copy-start.74 = (pred[320]{0:T(512)(128)(4,1)S(1)}, pred[320]{0:T(512)(128)(4,1)}, u32[]{:S(2)}) copy-start(pred[320]{0:T(512)(128)(4,1)} %get-tuple-element.356) | copy-start | bytes 964
  342.5 110.4 %copy-start.112 = (pred[320]{0:T(512)(128)(4,1)S(1)}, pred[320]{0:T(512)(128)(4,1)}, u32[]{:S(2)}) copy-start(pred[320]{0:T(512)(128)(4,1)} %get-tuple-element.354) | copy-start | bytes 964
  (84 other events, 478.0 us)
where the time goes:
time: 570 us; the launch traced here: 567 us
  blocking collectives  410 us (72%)
  local copies, waits for them, and re-layouts  94 us (16%)
  other arithmetic  34.3 us (6%)
  starting transfers between devices  17 us (3%)
  between operations  9.18 us (2%)
    psum x1, blocking collectives, on_device(): coarse_rhs = lax.psum(coarse_partial, ('gx', 'gy'))  109 us
    psum x1, blocking collectives, on_device(): lax.psum((precond_local, curvature_local, norm_local), ('gx', 'gy'))  102 us
    unnamed x1, blocking collectives  99.5 us
    psum x1, blocking collectives, on_device(): fresh_norm = lax.psum(jnp.sum(residual_out * residual_out), ('gx', 'gy'))  99.4 us
    mul x78, local copies, waits for them, and re-layouts, contract(): total = total + matrices[index][:, None, None, :] * moved[index][None]  28.3 us
    unnamed x280, local copies, waits for them, and re-layouts  12 us
    all_to_all x2, starting transfers between devices, face_sum(): lax.all_to_all(outgoing, 'gy', split_axis=1, concat_axis=1, tiled=True)  11.8 us
  transfers between devices with their start and end apart: 6, of which 0 were waited for; matrix products, arithmetic and copies ran while one was open for 12% of the time, Pallas kernels for 0%

commit v1 on v0

--- a/solution.py
+++ b/solution.py
@@ -134,7 +134,9 @@
         EDGE * EDGE, peer_count, capacity
     )
     own_index = lax.axis_index("gy")
-    arrived = lax.all_to_all(outgoing, "gy", split_axis=1, concat_axis=1, tiled=True)
+    pieces = jnp.split(outgoing, lax.axis_size("gy"), axis=1)
+    arrived_2 = lax.all_to_all(jnp.stack(pieces), "gy", 0, 0)
+    arrived = jnp.concatenate(arrived_2, axis=1)
     swapped = arrived.reshape(EDGE * EDGE, peer_count, capacity // 2, 2)[..., ::-1].reshape(
         EDGE * EDGE, peer_count, capacity
     )

time: 570 us -> 587 us (1.030)
  other arithmetic: 34.3 us -> 49.6 us
    mul x78, local copies, waits for them, and re-layouts: 28.3 us -> 16.5 us  [contract(): total = total + matrices[index][:, None, None, :] * moved[index][None]]
    select_n x0 -> x2, other arithmetic: none -> 6.09 us  [orient_columns(): jnp.where((orient_codes >= 4)[None, None, :], jnp.swapaxes(face_grid, 0,...]
    unnamed x280 -> x339, local copies, waits for them, and re-layouts: 12 us -> 15.2 us
  transfers between devices with their start and end apart: 6 -> 6, of which waited for: 0 -> 0; matrix products, arithmetic and copies ran while one was open for 12% -> 8% of each run, Pallas kernels for 0% -> 0%
where the time goes in v1:
time: 587 us; the launch traced here: 579 us
  blocking collectives  411 us (70%)
  local copies, waits for them, and re-layouts  89.7 us (15%)
  other arithmetic  49.6 us (8%)
  starting transfers between devices  16 us (3%)
  between operations  9.68 us (2%)
    psum x1, blocking collectives, on_device(): coarse_rhs = lax.psum(coarse_partial, ('gx', 'gy'))  109 us
    psum x1, blocking collectives, on_device(): lax.psum((precond_local, curvature_local, norm_local), ('gx', 'gy'))  103 us
    unnamed x1, blocking collectives  99.8 us
    psum x1, blocking collectives, on_device(): fresh_norm = lax.psum(jnp.sum(residual_out * residual_out), ('gx', 'gy'))  99 us
    mul x78, local copies, waits for them, and re-layouts, contract(): total = total + matrices[index][:, None, None, :] * moved[index][None]  16.5 us
    unnamed x339, local copies, waits for them, and re-layouts  15.2 us
  transfers between devices with their start and end apart: 6, of which 0 were waited for; matrix products, arithmetic and copies ran while one was open for 8% of the time, Pallas kernels for 0%

profile of v1, /device:TPU:1, one launch (start us, length us, event | category | flops | bytes accessed | tf_op | source)
XLA Modules:
  0.0 578.6 jit_solution(2032918064592078883)
XLA Ops:
  3.8 1.0 broadcast_multiply_fusion.3
  6.7 2.2 copy.409
  8.9 2.4 reshape.1881
  12.4 1.1 gather_fusion.1
  16.3 7.7 %all-to-all-start = ((f32[16,1,1280]{2,1,0:T(1,128)}), f32[16,1,1280]{2,1,0:T(1,128)S(1)}, u32[]{:S(2)}, u32[]{:S(2)}) async-start(f32[16,1,1280]{2,1,0:T(1,128)} %reshape.2006), calls=%async_computation | async-start | bytes 163840 | tf_op jit(solution)/shard_map/all_to_all | solution.py:138
  25.0 2.5 collective-permute-start
  30.2 5.9 %scatter_custom_fusion.1 = f32[8192]{0:T(1024)S(1)} fusion(s32[1024]{0:T(1024)S(1)} %bitcast.793, f32[1024]{0:T(1024)S(1)} %convolution_bitcast_fusion, f32[]{:T(128)} %constant.402.clone.1), kind=kCustom, calls=%fused_computation.229 | custom fusion | flops 1024 | bytes 32772 | tf_op jit(solution)/shard_map/scatter-add | solution.py:193
  36.2 109.2 %psum.35 = f32[8192]{0:T(1024)S(1)} all-reduce(f32[8192]{0:T(1024)S(1)} %scatter_custom_fusion.1), channel_id=1, replica_groups=mesh['gx'=32,'gy'=16] {'gx','gy'}, use_global_device_ids=true, to_apply=%region_2.5 | all-reduce | flops 8192 | bytes 65536 | tf_op jit(solution)/shard_map/psum | solution.py:196
  171.6 99.8 %all-reduce = f32[8192]{0:T(1024)S(1)} all-reduce(f32[8192]{0:T(1024)S(1)} %dynamic-update-slice.36), channel_id=1, replica_groups=mesh['gx'=32,'gy'=16] {'gx','gy'}, use_global_device_ids=true, to_apply=%add | all-reduce | flops 8192 | bytes 65536
  271.4 6.1 %gather_fusion = f32[1024]{0:T(1024)S(1)} fusion(f32[8192]{0:T(1024)S(1)} %all-reduce, s32[1024]{0:T(1024)S(1)} %fusion.34), kind=kCustom, calls=%fused_computation.4 | custom fusion | bytes 12288 | tf_op jit(solution)/shard_map/gather | solution.py:203
  279.4 1.4 reshape.1998
  280.8 2.2 broadcast_select_fusion.1
  283.0 1.7 rev.31
  284.7 2.2 broadcast_select_fusion.3
  286.9 2.0 rev.32
  288.9 2.2 broadcast_select_fusion.5
  291.8 1.9 bitcast_select_fusion
  293.7 1.7 copy.416
  295.7 2.9 scatter_custom_fusion
  298.6 1.9 reshape.1889
  300.5 1.7 fusion.48
  302.3 1.3 copy.486
  303.6 1.2 copy.487
  304.8 1.2 copy.424
  308.4 1.2 multiply_reduce_fusion
  317.3 2.0 copy.451
  319.4 1.6 reshape.1899
  321.0 2.1 gather_fusion.3
  323.1 1.8 gather_fusion.4
  325.4 1.0 reduce.28
  327.2 4.0 all-to-all-start.1
  331.4 1.5 collective-permute-start.2
  335.7 2.9 add_reduce_fusion
  339.8 103.4 %all-reduce.2 = (f32[]{:T(128)}, f32[]{:T(128)}) all-reduce(f32[]{:T(128)} %get-tuple-element.150, f32[]{:T(128)S(6)} %add.970), channel_id=1, replica_groups=mesh['gx'=32,'gy'=16] {'gx','gy'}, use_global_device_ids=true, to_apply=%region_4.7 | all-reduce | flops 2 | bytes 16 | tf_op jit(solution)/shard_map/psum | solution.py:209
  447.0 1.5 reshape.1999
  448.5 2.2 broadcast_select_fusion
  450.7 1.7 rev.36
  452.3 2.2 broadcast_select_fusion.2
  455.5 1.9 fusion.1
  457.4 2.8 copy.457
  460.2 4.2 broadcast_select_fusion.6
  464.4 1.7 copy.458
  466.4 2.3 scatter_custom_fusion.2
  469.6 1.7 fusion.47
  471.3 1.3 copy.492
  472.7 1.3 copy.493
  475.5 1.3 multiply_reduce_fusion.1
  476.9 99.0 %all-reduce.1 = (f32[]{:T(128)}, f32[]{:T(128)}) all-reduce(f32[]{:T(128)} %get-tuple-element.156, f32[]{:T(128)} %get-tuple-element.149), channel_id=1, replica_groups=mesh['gx'=32,'gy'=16] {'gx','gy'}, use_global_device_ids=true, to_apply=%region_11.14 | all-reduce | flops 2 | bytes 16 | tf_op jit(solution)/shard_map/psum | solution.py:214
  (575 shorter events, 58.8 us)
Async XLA Ops:
  0.6 148.2 %copy-start = (f32[16,8192]{1,0:T(8,128)S(1)}, f32[16,8192]{1,0:T(8,128)}, u32[]{:S(2)}) copy-start(f32[16,8192]{1,0:T(8,128)} %param.48) | copy-start | bytes 1572868
  4.8 25.2 %copy-start.2 = (f32[512,128]{1,0:T(8,128)}, f32[512,128]{1,0:T(8,128)S(1)}, u32[]{:S(2)}) copy-start(f32[512,128]{1,0:T(8,128)S(1)} %broadcast_multiply_fusion.3) | copy-start | bytes 786436
  12.2 3.2 copy-start.129
  12.3 3.1 copy-start.131
  12.4 3.1 copy-start.76
  12.4 11.6 %copy-start.122 = (s32[1024]{0:T(1024)}, s32[1024]{0:T(1024)S(1)}, u32[]{:S(2)}) copy-start(s32[1024]{0:T(1024)S(1)} %get-tuple-element.377) | copy-start | bytes 12292
  13.5 11.2 %copy-start.138 = (s32[1,2,64]{2,1,0:T(2,128)S(1)}, s32[1,2,64]{2,1,0:T(2,128)}, u32[]{:S(2)}) copy-start(s32[1,2,64]{2,1,0:T(2,128)} %param.53) | copy-start | bytes 1540
  15.5 14.7 %copy-start.137 = (s32[8,128]{1,0:T(8,128)S(1)}, s32[8,128]{1,0:T(8,128)}, u32[]{:S(2)}) copy-start(s32[8,128]{1,0:T(8,128)} %param.47) | copy-start | bytes 12292
  16.3 129.4 %copy-start.5 = (bf16[3,512,128]{2,1,0:T(8,128)(2,1)S(1)}, bf16[3,512,128]{2,1,0:T(8,128)(2,1)}, u32[]{:S(2)}) copy-start(bf16[3,512,128]{2,1,0:T(8,128)(2,1)} %param.44) | copy-start | bytes 1179652
  16.3 261.5 %all-to-all-start = ((f32[16,1,1280]{2,1,0:T(1,128)}), f32[16,1,1280]{2,1,0:T(1,128)S(1)}, u32[]{:S(2)}, u32[]{:S(2)}) async-start(f32[16,1,1280]{2,1,0:T(1,128)} %reshape.2006), calls=%async_computation | async-start | bytes 163840 | tf_op jit(solution)/shard_map/all_to_all | solution.py:138
  24.8 3.1 copy-start.135
  24.8 252.9 %copy-start.74 = (pred[128]{0:T(512)(128)(4,1)}, pred[128]{0:T(512)(128)(4,1)S(1)}, u32[]{:S(2)}) copy-start(pred[128]{0:T(512)(128)(4,1)S(1)} %get-tuple-element.364) | copy-start | bytes 388
  24.8 252.9 %copy-start.95 = (pred[128]{0:T(512)(128)(4,1)}, pred[128]{0:T(512)(128)(4,1)S(1)}, u32[]{:S(2)}) copy-start(pred[128]{0:T(512)(128)(4,1)S(1)} %get-tuple-element.365) | copy-start | bytes 388
  24.8 252.9 %copy-start.133 = (pred[128]{0:T(512)(128)(4,1)}, pred[128]{0:T(512)(128)(4,1)S(1)}, u32[]{:S(2)}) copy-start(pred[128]{0:T(512)(128)(4,1)S(1)} %get-tuple-element.363) | copy-start | bytes 388
  25.0 252.6 %collective-permute-start = (f32[64,1,64]{2,0,1:T(8,128)S(1)}, f32[64,1,64]{2,0,1:T(8,128)S(1)}, u32[]{:S(2)}, u32[]{:S(2)}) collective-permute-start(f32[64,1,64]{2,0,1:T(8,128)S(1)} %copy.484), channel_id=1, source_target_pairs={{0,16},{16,32},{32,48},{48,64},{64,80},{80,96},{96,112},{112,128},... | collective-permute-start | bytes 49160 | tf_op jit(solution)/shard_map/ppermute | solution.py:16
  27.6 250.0 %collective-permute-start.1 = (f32[64,1,64]{2,0,1:T(8,128)S(1)}, f32[64,1,64]{2,0,1:T(8,128)S(1)}, u32[]{:S(2)}, u32[]{:S(2)}) collective-permute-start(f32[64,1,64]{2,0,1:T(8,128)S(1)} %copy.485), channel_id=1, source_target_pairs={{16,0},{32,16},{48,32},{64,48},{80,64},{96,80},{112,96},{128,112},... | collective-permute-start | bytes 49160 | tf_op jit(solution)/shard_map/ppermute | solution.py:19
  29.5 117.1 %copy-start.4 = (bf16[3,512,128]{2,1,0:T(8,128)(2,1)S(1)}, bf16[3,512,128]{2,1,0:T(8,128)(2,1)}, u32[]{:S(2)}) copy-start(bf16[3,512,128]{2,1,0:T(8,128)(2,1)} %param.43) | copy-start | bytes 1179652
  145.7 21.0 %copy-start.71 = (f32[8]{0:T(128)}, f32[8]{0:T(128)S(1)}, u32[]{:S(2)}) copy-start(f32[8]{0:T(128)S(1)} %get-tuple-element.357) | copy-start | bytes 100
  145.7 21.7 %copy-start.69 = (f32[8]{0:T(128)}, f32[8]{0:T(128)S(1)}, u32[]{:S(2)}) copy-start(f32[8]{0:T(128)S(1)} %get-tuple-element.356) | copy-start | bytes 100
  145.7 22.3 %copy-start.67 = (f32[8]{0:T(128)}, f32[8]{0:T(128)S(1)}, u32[]{:S(2)}) copy-start(f32[8]{0:T(128)S(1)} %get-tuple-element.355) | copy-start | bytes 100
  145.7 23.0 %copy-start.65 = (f32[8]{0:T(128)}, f32[8]{0:T(128)S(1)}, u32[]{:S(2)}) copy-start(f32[8]{0:T(128)S(1)} %get-tuple-element.354) | copy-start | bytes 100
  302.2 3.8 copy-start.19
  302.2 4.0 copy-start.18
  302.2 4.2 copy-start.16
  303.6 3.1 copy-start.79
  303.6 3.1 copy-start.80
  313.5 3.2 copy-start.6
  319.4 5.5 copy-start.130
  319.4 5.5 copy-start.132
  323.0 8.1 %copy-start.136 = (pred[128]{0:T(512)(128)(4,1)S(1)}, pred[128]{0:T(512)(128)(4,1)}, u32[]{:S(2)}) copy-start(pred[128]{0:T(512)(128)(4,1)} %copy-done.135) | copy-start | bytes 388
  324.8 8.2 %copy-start.57 = (f32[8,8,128]{2,1,0:T(8,128)S(1)}, f32[8,8,128]{2,1,0:T(8,128)}, u32[]{:S(2)}) copy-start(f32[8,8,128]{2,1,0:T(8,128)} %copy-done.56) | copy-start | bytes 98308
  325.0 8.0 %copy-start.53 = (f32[8,8,128]{2,1,0:T(8,128)S(1)}, f32[8,8,128]{2,1,0:T(8,128)}, u32[]{:S(2)}) copy-start(f32[8,8,128]{2,1,0:T(8,128)} %copy-done.52) | copy-start | bytes 98308
  325.0 8.0 %copy-start.49 = (f32[8,8,128]{2,1,0:T(8,128)S(1)}, f32[8,8,128]{2,1,0:T(8,128)}, u32[]{:S(2)}) copy-start(f32[8,8,128]{2,1,0:T(8,128)} %copy-done.48) | copy-start | bytes 98308
  325.1 8.0 %copy-start.45 = (f32[8,8,128]{2,1,0:T(8,128)S(1)}, f32[8,8,128]{2,1,0:T(8,128)}, u32[]{:S(2)}) copy-start(f32[8,8,128]{2,1,0:T(8,128)} %copy-done.44) | copy-start | bytes 98308
  325.2 7.9 %copy-start.41 = (f32[8,8,128]{2,1,0:T(8,128)S(1)}, f32[8,8,128]{2,1,0:T(8,128)}, u32[]{:S(2)}) copy-start(f32[8,8,128]{2,1,0:T(8,128)} %copy-done.40) | copy-start | bytes 98308
  325.4 7.8 %copy-start.37 = (f32[8,8,128]{2,1,0:T(8,128)S(1)}, f32[8,8,128]{2,1,0:T(8,128)}, u32[]{:S(2)}) copy-start(f32[8,8,128]{2,1,0:T(8,128)} %copy-done.36) | copy-start | bytes 98308
  326.4 6.9 %copy-start.35 = (f32[8,8,128]{2,1,0:T(8,128)S(1)}, f32[8,8,128]{2,1,0:T(8,128)}, u32[]{:S(2)}) copy-start(f32[8,8,128]{2,1,0:T(8,128)} %copy-done.34) | copy-start | bytes 98308
  327.2 6.1 %copy-start.33 = (f32[8,8,128]{2,1,0:T(8,128)S(1)}, f32[8,8,128]{2,1,0:T(8,128)}, u32[]{:S(2)}) copy-start(f32[8,8,128]{2,1,0:T(8,128)} %copy-done.32) | copy-start | bytes 98308
  327.2 118.2 %all-to-all-start.1 = ((f32[16,1,1280]{2,1,0:T(1,128)}), f32[16,1,1280]{2,1,0:T(1,128)S(1)}, u32[]{:S(2)}, u32[]{:S(2)}) async-start(f32[16,1,1280]{2,1,0:T(1,128)} %reshape.2008), calls=%async_computation.1 | async-start | bytes 163840 | tf_op jit(solution)/shard_map/all_to_all | solution.py:138
  331.4 113.8 %collective-permute-start.2 = (f32[64,1,64]{2,0,1:T(8,128)S(1)}, f32[64,1,64]{2,0,1:T(8,128)S(1)}, u32[]{:S(2)}, u32[]{:S(2)}) collective-permute-start(f32[64,1,64]{2,0,1:T(8,128)S(1)} %copy.490), channel_id=1, source_target_pairs={{0,16},{16,32},{32,48},{48,64},{64,80},{80,96},{96,112},{112,128},... | collective-permute-start | bytes 49160 | tf_op jit(solution)/shard_map/ppermute | solution.py:16
  333.0 112.2 %collective-permute-start.3 = (f32[64,1,64]{2,0,1:T(8,128)S(1)}, f32[64,1,64]{2,0,1:T(8,128)S(1)}, u32[]{:S(2)}, u32[]{:S(2)}) collective-permute-start(f32[64,1,64]{2,0,1:T(8,128)S(1)} %copy.491), channel_id=1, source_target_pairs={{16,0},{32,16},{48,32},{64,48},{80,64},{96,80},{112,96},{128,112},... | collective-permute-start | bytes 49160 | tf_op jit(solution)/shard_map/ppermute | solution.py:19
  335.7 108.8 %copy-start.64 = (f32[512,128]{1,0:T(8,128)S(1)}, f32[512,128]{1,0:T(8,128)}, u32[]{:S(2)}) copy-start(f32[512,128]{1,0:T(8,128)} %param.41) | copy-start | bytes 786436
  335.7 108.8 %copy-start.84 = (f32[128]{0:T(128)S(1)}, f32[128]{0:T(128)}, u32[]{:S(2)}) copy-start(f32[128]{0:T(128)} %copy-done.82) | copy-start | bytes 1540
  335.7 109.6 %copy-start.75 = (pred[128]{0:T(512)(128)(4,1)S(1)}, pred[128]{0:T(512)(128)(4,1)}, u32[]{:S(2)}) copy-start(pred[128]{0:T(512)(128)(4,1)} %copy-done.74) | copy-start | bytes 388
  335.7 109.6 %copy-start.96 = (pred[128]{0:T(512)(128)(4,1)S(1)}, pred[128]{0:T(512)(128)(4,1)}, u32[]{:S(2)}) copy-start(pred[128]{0:T(512)(128)(4,1)} %copy-done.95) | copy-start | bytes 388
  335.7 109.6 %copy-start.134 = (pred[128]{0:T(512)(128)(4,1)S(1)}, pred[128]{0:T(512)(128)(4,1)}, u32[]{:S(2)}) copy-start(pred[128]{0:T(512)(128)(4,1)} %copy-done.133) | copy-start | bytes 388
  471.3 3.5 copy-start.14
  474.8 102.4 %copy-start.1 = (f32[16,8192]{1,0:T(8,128)S(1)}, f32[16,8192]{1,0:T(8,128)}, u32[]{:S(2)}) copy-start(f32[16,8192]{1,0:T(8,128)} %param.48) | copy-start | bytes 1572868
  (98 other events, 156.3 us)
